TPU v7x, 512 devices: a whole 4x4x16 slice. The times are simulated.
512 devices in a mesh: dp: 4 (over x), head: 8 (over y, core), seq: 16 (over z).
Axes of the slice: x: 4, y: 4, z: 16, core: 2. Of those that a mesh axis runs over, the one named last changes fastest.
Arguments:
- queries: bfloat16 [32768, 3072], P(('dp', 'seq'), 'head'), parts along dimension 0, may hold values from -58 to 58
- keys: bfloat16 [32768, 3072], P(('dp', 'seq'), 'head'), parts along dimension 0, may hold values from -6 to 6
- values: bfloat16 [32768, 3072], P(('dp', 'seq'), 'head'), parts along dimension 0, may hold values from -16 to 16
- indices: int32 [24, 512, 32], P('head', ('dp', 'seq')), parts along dimension 1, may hold values from 0 to 127, as said below
Outputs:
- attended: bfloat16 [32768, 3072], P(('dp', 'seq'), 'head'), parts along dimension 0
There are 4 independent parts, one for each index of `dp`. A program takes and returns all parts, laid end to end along the dimension named above; each array names one. Nothing has to cross between parts.
Inputs may be any that keep to these rules, and one draw needn't show every extreme that they name: The 32 entries of indices[h, c] are distinct. For one head and the query cubes of one aligned block of 8 cubes, the distinct key cubes they select inside any one aligned block of 8 cubes number at most 3.
All inputs are finite; a program needn't handle non-finite values.
Results may differ from a plain program's by a relative error of at most 0.008.
Values may be sent and summed in bfloat16 or wider, within the bound.
A program may use at most 192 MiB of HBM per device.

v0:
```python
import math

import jax
import jax.numpy as jnp
from jax import lax
from jax.sharding import PartitionSpec as P

CUBE_TOK = 64


NEG_FILL = -1e30


def cube_major(block, heads):
    tokens, width = block.shape
    return block.reshape(tokens // CUBE_TOK, CUBE_TOK, heads, width // heads)


def merge_parts(first, second):
    highest = jnp.maximum(first[0], second[0])
    right_scale = jnp.exp(second[0] - highest)
    totals = second[1] * right_scale
    mixed = second[2] * right_scale[..., None]
    return (highest, totals, mixed)


def body(queries, keys, values, indices):
    heads = indices.shape[0]
    cube_dev = indices.shape[1]
    depth = queries.shape[1] // heads
    factor = 1.0 / math.sqrt(depth)
    query_cubes = cube_major(queries, heads)
    start_state = (
        jnp.full((cube_dev, CUBE_TOK, heads), NEG_FILL, jnp.float32),
        jnp.zeros((cube_dev, CUBE_TOK, heads), jnp.float32),
        jnp.zeros((cube_dev, CUBE_TOK, heads, depth), jnp.float32),
    )
    key_piece = cube_major(lax.all_gather(keys, "seq", axis=0, tiled=True), heads)
    value_piece = cube_major(lax.all_gather(values, "seq", axis=0, tiled=True), heads)
    width = key_piece.shape[0]
    inside = jnp.any(indices[..., None] == jnp.arange(width, dtype=jnp.int32), axis=2)
    usable = inside.transpose(1, 0, 2)[:, None, :, :, None]
    scores = (
        jnp.einsum("cqhd,kuhd->cqhku", query_cubes, key_piece, preferred_element_type=jnp.float32)
        * factor
    )
    scores = jnp.where(usable, scores, NEG_FILL)
    highest = jnp.max(scores, axis=(3, 4))
    weights = jnp.where(usable, jnp.exp(scores - highest[..., None, None]), 0.0)
    totals = jnp.sum(weights, axis=(3, 4))
    mixed = jnp.einsum(
        "cqhku,kuhd->cqhd",
        weights.astype(jnp.bfloat16),
        value_piece,
        preferred_element_type=jnp.float32,
    )
    highest, totals, mixed = merge_parts(start_state, (highest, totals, mixed))
    result = (mixed / totals[..., None]).astype(jnp.bfloat16)
    return result.reshape(queries.shape)


def solution(mesh):
    placed = (
        P(("dp", "seq"), "head"),
        P(("dp", "seq"), "head"),
        P(("dp", "seq"), "head"),
        P("head", ("dp", "seq"), None),
    )
    return jax.shard_map(
        body, mesh=mesh, in_specs=placed, out_specs=P(("dp", "seq"), "head"), check_vma=False
    )
```

profile of v0, /device:TPU:16, one launch (start us, length us, event | category | flops | bytes accessed | tf_op | source)
XLA Modules:
  0.0 258.0 jit_solution(12128518731981042703)
XLA Ops:
  6.5 0.0 all-gather.3.cloned.1.call-start
  6.5 0.7 all-gather.3.cloned.1.call-update
  7.3 0.0 all-gather.5.cloned.1.call-start
  7.3 0.7 all-gather.5.cloned.1.call-update
  8.0 1.4 reshape.26
  9.4 0.9 fusion.31
  10.3 89.8 %all-gather.3.cloned.1.call-done = bf16[8192,384]{1,0:T(8,128)(2,1)} async-done(((bf16[512,384]{1,0:T(8,128)(2,1)}), bf16[8192,384]{1,0:T(8,128)(2,1)}) %all-gather.3.cloned.1.call-update) | async-done | bytes 6291472 | tf_op jit(solution)/shard_map/all_gather | solution.py:38
  100.1 16.7 %reshape.25 = bf16[128,64,3,128]{3,2,1,0:T(4,128)(2,1)} reshape(bf16[8192,384]{1,0:T(8,128)(2,1)} %all-gather.3.cloned.1.call-done) | data formatting | bytes 12582912 | tf_op jit(solution)/shard_map/reshape | solution.py:16
  116.7 50.0 %fusion = (f32[8,64,3]{1,0,2:T(8,128)S(1)}, f32[3,128,64,8,64]{1,4,3,2,0:T(8,128)}) fusion(pred[8,3,128]{2,0,1:T(8,128)(4,1)S(1)} %bitcast.56, bf16[8,64,3,128,1]{3,2,1,0,4:T(4,128)(2,1)S(1)} %bitcast.55, bf16[128,64,3,128,1]{3,2,1,0,4:T(4,128)(2,1)} %bitcast.52), kind=kOutput, calls=%fused_computation.2 | convolution fusion | flops 3258972672 | bytes 57025536 | tf_op jit(solution)/shard_map/cqhd,kuhd->cqhku/dot_general | solution.py:44
  166.7 22.2 %fusion.1 = f32[8,64,3]{1,0,2:T(8,128)S(1)} fusion(f32[3,128,64,8,64]{1,4,3,2,0:T(8,128)} %get-tuple-element.8, f32[8,64,3]{1,0,2:T(8,128)S(1)} %get-tuple-element.7, pred[8,3,128]{2,0,1:T(8,128)(4,1)S(1)} %bitcast.57), kind=kLoop, calls=%fused_computation.3 | loop fusion | flops 62913024 | bytes 50347008 | tf_op jit(solution)/shard_map/reduce_sum | solution.py:50
  188.9 0.0 all-gather.5.cloned.1.call-done
  188.9 16.6 %reshape.27 = bf16[128,64,3,128]{3,2,1,0:T(4,128)(2,1)} reshape(bf16[8192,384]{1,0:T(8,128)(2,1)} %all-gather.5.cloned.1.call-done) | data formatting | bytes 12582912 | tf_op jit(solution)/shard_map/reshape | solution.py:16
  205.6 44.4 %fusion.25 = bf16[8,64,3,128]{3,1,0,2:T(8,128)(2,1)S(1)} fusion(bf16[128,64,3,128,1]{3,2,1,0,4:T(4,128)(2,1)} %bitcast.53, f32[3,128,64,8,64]{1,4,3,2,0:T(8,128)} %get-tuple-element.8, f32[8,64,3]{1,0,2:T(8,128)S(1)} %get-tuple-element.7, pred[8,3,128]{2,0,1:T(8,128)(4,1)S(1)} %bitcast.58, f32[8,64,3]{1,0,2:T(8,128)S(1)} %get-tuple-element.6, ...), kind=kOutput, calls=%fused_computation.14 | convolution fusion | flops 3284729856 | bytes 57037824 | tf_op jit(solution)/shard_map/cqhku,kuhd->cqhd/dot_general | solution.py:51
  250.0 0.3 copy.16
  250.3 0.8 copy.49
  (1 shorter events, 0.0 us)
Async XLA Ops:
  6.5 93.5 %all-gather.3.cloned.1.call-start = ((), (), s32[]{:S(2)}) async-start(), calls=%async_computation | async-start | bytes 6684672 | tf_op jit(solution)/shard_map/all_gather | solution.py:38
  7.3 181.7 %all-gather.5.cloned.1.call-start = ((), (), s32[]{:S(2)}) async-start(), calls=%async_computation.1 | async-start | bytes 6684672 | tf_op jit(solution)/shard_map/all_gather | solution.py:39
Sparse Core Ops, SparseCore 0:
  9.4 90.5 all-gather.2
  102.1 82.8 all-gather.4
where the time goes:
time: 259 us; the launch traced here: 258 us
  matrix products  94.4 us (36%)
  waiting for transfers between devices  91.2 us (35%)
  local copies, waits for them, and re-layouts  35.8 us (14%)
  other arithmetic  23.1 us (9%)
  between operations  13.4 us (5%)
    all_gather x1, waiting for transfers between devices, body(): lax.all_gather(keys, 'seq', axis=0, tiled=True)  89.8 us
    dot_general x1, matrix products, body(): jnp.einsum('cqhd,kuhd->cqhku', query_cubes, key_piece, preferred_element_...  50 us
    dot_general x1, matrix products, body(): jnp.einsum('cqhku,kuhd->cqhd', weights.astype(jnp.bfloat16), value_piece,...  44.4 us
    reshape x3, local copies, waits for them, and re-layouts, cube_major(): return block.reshape(tokens // CUBE_TOK, CUBE_TOK, heads, width // heads)  34.7 us
    reduce_sum x1, other arithmetic, body(): totals = jnp.sum(weights, axis=(3, 4))  22.2 us
  transfers between devices with their start and end apart: 2, of which 1 were waited for; matrix products, arithmetic and copies ran while one was open for 35% of the time, Pallas kernels for 0%

commit v1 on v0

v1 whole, which is shorter than its diff:
```python
import functools
import math

import jax
import jax.numpy as jnp
from jax import lax
from jax.experimental import pallas as pl
from jax.experimental.pallas import tpu as pltpu
from jax.sharding import PartitionSpec as P

CUBE_TOK = 64
LANES = 128
MASKED = -1e30
RIGHT, LEFT = 0, 1


def kernel(ring_size, q_hbm, k_hbm, v_hbm, idx_ref, out_ref,
           q_aug, ring, acc, top, tot, q_sem, kv_sem, send_sem, recv_sem):
    heads = idx_ref.shape[0]
    cubes = idx_ref.shape[1]
    picks = idx_ref.shape[2]
    rows = q_hbm.shape[0]
    depth = q_hbm.shape[1] // heads
    half = ring_size // 2
    factor = math.log2(math.e) / math.sqrt(depth)
    me = lax.axis_index("seq")
    right = lax.rem(me + 1, ring_size)
    left = lax.rem(me + ring_size - 1, ring_size)

    barrier = pltpu.get_barrier_semaphore()
    for neighbour in (left, right):
        pl.semaphore_signal(barrier, inc=1, device_id={"seq": neighbour},
                            device_id_type=pl.DeviceIdType.MESH)

    loads = []
    for h in range(heads):
        columns = pl.ds(h * depth, depth)
        for part, ref in ((0, k_hbm), (1, v_hbm)):
            loads.append(pltpu.make_async_copy(
                ref.at[:, columns], ring.at[RIGHT, 0, h, part], kv_sem.at[h, part]))
            loads[-1].start()
    q_loads = []
    for h in range(heads):
        q_loads.append(pltpu.make_async_copy(
            q_hbm.at[:, pl.ds(h * depth, depth)], q_aug.at[h, :, pl.ds(0, depth)], q_sem.at[h]))
        q_loads[-1].start()

    def hop(way, step, h):
        return pltpu.make_async_remote_copy(
            src_ref=ring.at[way, step, h],
            dst_ref=ring.at[way, step + 1, h],
            send_sem=send_sem.at[way, step, h],
            recv_sem=recv_sem.at[way, step, h],
            device_id={"seq": right if way == RIGHT else left},
            device_id_type=pl.DeviceIdType.MESH)

    def first_hop(way, h):
        return pltpu.make_async_remote_copy(
            src_ref=ring.at[RIGHT, 0, h],
            dst_ref=ring.at[way, 1, h],
            send_sem=send_sem.at[way, 0, h],
            recv_sem=recv_sem.at[way, 0, h],
            device_id={"seq": right if way == RIGHT else left},
            device_id_type=pl.DeviceIdType.MESH)

    def last_hop(way, h):
        part = 0 if way == RIGHT else 1
        return pltpu.make_async_remote_copy(
            src_ref=ring.at[way, half - 1, h, part],
            dst_ref=ring.at[way, half, h, part],
            send_sem=send_sem.at[way, half - 1, h],
            recv_sem=recv_sem.at[way, half - 1, h],
            device_id={"seq": right if way == RIGHT else left},
            device_id_type=pl.DeviceIdType.MESH)

    pl.semaphore_wait(barrier, 2)
    for h in range(heads):
        loads[2 * h].wait()
        loads[2 * h + 1].wait()
        first_hop(RIGHT, h).start()
        first_hop(LEFT, h).start()

    lanes = lax.broadcasted_iota(jnp.int32, (cubes, LANES), 1)
    for h in range(heads):
        chosen = idx_ref[h]
        hit = jnp.zeros((cubes, LANES), jnp.float32)
        for j in range(picks):
            hit = jnp.where(chosen[:, j:j + 1] == lanes, 1.0, hit)
        bias = jnp.where(hit > 0.5, 0.0, MASKED)
        for c in range(cubes):
            q_aug[h, c * CUBE_TOK:(c + 1) * CUBE_TOK, depth:] = jnp.broadcast_to(
                bias[c:c + 1, :], (CUBE_TOK, LANES)).astype(q_aug.dtype)
    top[...] = jnp.full(top.shape, MASKED, jnp.float32)
    tot[...] = jnp.zeros(tot.shape, jnp.float32)
    acc[...] = jnp.zeros(acc.shape, jnp.float32)
    for h in range(heads):
        q_loads[h].wait()

    key_cube = lax.shift_right_logical(
        lax.broadcasted_iota(jnp.int32, (rows, LANES), 0), jnp.int32(6))
    key_lane = lax.broadcasted_iota(jnp.int32, (rows, LANES), 1)

    def one_hot(owner):
        return jnp.where(key_lane == key_cube + owner * cubes, 1.0, 0.0).astype(jnp.bfloat16)

    tile = min(rows, 256)

    def attend(h, blocks):
        wide = [jnp.concatenate([key[...], hot], axis=1) for key, _, hot in blocks]
        for r in range(0, rows, tile):
            part = pl.ds(r, tile)
            scores = [
                lax.dot_general(q_aug[h, part, :], k, (((1,), (1,)), ((), ())),
                                preferred_element_type=jnp.float32)
                for k in wide
            ]
            peak = jnp.max(functools.reduce(jnp.maximum, scores), axis=1, keepdims=True)
            before = top[h, part, :]
            after = jnp.maximum(before, peak)
            scale = jnp.exp2((before - after) * factor)
            total = tot[h, part, :] * scale
            mixed = acc[h, part, :] * scale
            for s, (_, value, _) in zip(scores, blocks):
                pieces = []
                for c in range(0, s.shape[1], LANES):
                    w = jnp.exp2((s[:, c:c + LANES] - after) * factor)
                    total = total + w
                    pieces.append(w.astype(jnp.bfloat16))
                mixed = mixed + jnp.dot(jnp.concatenate(pieces, axis=1), value[...],
                                        preferred_element_type=jnp.float32)
            top[h, part, :] = after
            tot[h, part, :] = total
            acc[h, part, :] = mixed

    hot_own = one_hot(me)
    for h in range(heads):
        attend(h, [(ring.at[RIGHT, 0, h, 0], ring.at[RIGHT, 0, h, 1], hot_own)])

    def body(step, carry):
        hot_r = one_hot(lax.rem(me - step + ring_size, ring_size))
        hot_l = one_hot(lax.rem(me + step, ring_size))
        for h in range(heads):
            for way in (RIGHT, LEFT):
                hop(way, step - 1, h).wait_recv()

                @pl.when(step < half - 1)
                def _():
                    hop(way, step, h).start()

                @pl.when(step == half - 1)
                def _():
                    last_hop(way, h).start()

            attend(h, [
                (ring.at[RIGHT, step, h, 0], ring.at[RIGHT, step, h, 1], hot_r),
                (ring.at[LEFT, step, h, 0], ring.at[LEFT, step, h, 1], hot_l),
            ])
        return carry

    lax.fori_loop(1, half, body, 0)

    hot_far = one_hot(lax.rem(me + half, ring_size))
    for h in range(heads):
        last_hop(RIGHT, h).wait_recv()
        last_hop(LEFT, h).wait_recv()
        attend(h, [(ring.at[RIGHT, half, h, 0], ring.at[LEFT, half, h, 1], hot_far)])
        total = jnp.sum(tot[h], axis=1, keepdims=True)
        out_ref[:, h * depth:(h + 1) * depth] = (acc[h] / total).astype(out_ref.dtype)

    for way in (RIGHT, LEFT):
        for h in range(heads):
            first_hop(way, h).wait_send()
            last_hop(way, h).wait_send()

    def drain(step, carry):
        for way in (RIGHT, LEFT):
            for h in range(heads):
                hop(way, step, h).wait_send()
        return carry

    lax.fori_loop(1, half - 1, drain, 0)


def body(ring_size, queries, keys, values, indices):
    heads = indices.shape[0]
    rows, width = queries.shape
    depth = width // heads
    half = ring_size // 2
    vmem = pl.BlockSpec(memory_space=pltpu.VMEM)
    hbm = pl.BlockSpec(memory_space=pl.ANY)
    return pl.pallas_call(
        functools.partial(kernel, ring_size),
        out_shape=jax.ShapeDtypeStruct((rows, width), queries.dtype),
        in_specs=[hbm, hbm, hbm, vmem],
        out_specs=vmem,
        scratch_shapes=[
            pltpu.VMEM((heads, rows, depth + LANES), jnp.bfloat16),
            pltpu.VMEM((2, half + 1, heads, 2, rows, depth), jnp.bfloat16),
            pltpu.VMEM((heads, rows, depth), jnp.float32),
            pltpu.VMEM((heads, rows, LANES), jnp.float32),
            pltpu.VMEM((heads, rows, LANES), jnp.float32),
            pltpu.SemaphoreType.DMA((heads,)),
            pltpu.SemaphoreType.DMA((heads, 2)),
            pltpu.SemaphoreType.DMA((2, half, heads)),
            pltpu.SemaphoreType.DMA((2, half, heads)),
        ],
        compiler_params=pltpu.CompilerParams(
            collective_id=0, has_side_effects=True, vmem_limit_bytes=48 * 2 ** 20),
        cost_estimate=pl.CostEstimate(
            flops=4 * rows * rows * ring_size * width,
            bytes_accessed=8 * rows * width,
            transcendentals=rows * rows * ring_size * heads),
        name="ring_attention",
    )(queries, keys, values, indices)


def solution(mesh):
    placed = (
        P(("dp", "seq"), "head"),
        P(("dp", "seq"), "head"),
        P(("dp", "seq"), "head"),
        P("head", ("dp", "seq"), None),
    )
    return jax.shard_map(
        functools.partial(body, mesh.shape["seq"]), mesh=mesh, in_specs=placed,
        out_specs=P(("dp", "seq"), "head"), check_vma=False,
    )
```

time: 259 us -> 145 us (0.56)
  the two profiles are of different devices: /device:TPU:16 before, /device:TPU:30 now
where the time goes in v1:
time: 145 us; the launch traced here: 144 us
  Pallas kernels  140 us (97%)
  local copies, waits for them, and re-layouts  4.44 us (3%)
    pallas_call x1, Pallas kernels, body(): pl.pallas_call(functools.partial(kernel, ring_size), out_shape=jax.ShapeD...  140 us
    unnamed x9, local copies, waits for them, and re-layouts  4.44 us

profile of v1, /device:TPU:30, one launch (start us, length us, event | category | flops | bytes accessed | tf_op | source)
XLA Modules:
  0.0 144.3 jit_solution(15690607408310622438)
XLA Ops:
  0.0 0.0 copy-start
  0.0 1.0 copy-done
  1.0 0.0 copy-start.1
  1.0 1.0 copy-done.1
  2.0 0.0 copy-start.2
  2.0 1.0 copy-done.2
  3.0 0.0 copy-start.3
  3.0 0.7 copy-done.3
  3.7 139.9 %ring_attention.1 = bf16[512,384]{1,0:T(8,128)(2,1)S(1)} custom-call(bf16[512,384]{1,0:T(8,128)(2,1)S(1)} %copy-done, bf16[512,384]{1,0:T(8,128)(2,1)S(1)} %copy-done.1, bf16[512,384]{1,0:T(8,128)(2,1)S(1)} %copy-done.2, s32[3,8,32]{2,1,0:T(8,128)S(1)} %copy-done.3), custom_call_target="tpu_custom_call" | custom-call | flops 6442450944 | bytes 1572864 | tf_op jit(solution)/shard_map/ring_attention/pallas_call | solution.py:191
  143.6 0.7 copy.6
Async XLA Ops:
  0.0 1.0 copy-start
  1.0 1.0 copy-start.1
  2.0 1.0 copy-start.2
  3.0 0.7 copy-start.3

commit v2 on v1

v2 whole, which is shorter than its diff:
```python
import functools
import math

import jax
import jax.numpy as jnp
from jax import lax
from jax.experimental import pallas as pl
from jax.experimental.pallas import tpu as pltpu
from jax.sharding import PartitionSpec as P

CUBE_TOK = 64
LANES = 128
MASKED = -1e30
KEEP = 3
PICKED = 16
NEAR = (1, -1, 2, -2)
RIGHT, LEFT = 0, 1
SHORT, LONG = 0, 1


def kernel(ring_size, q_hbm, k_hbm, v_hbm, idx_hbm, out_ref,
           q_aug, ring, stage, pairs, single, marks, tables, idx_ref, acc, top, tot,
           q_sem, kv_sem, idx_sem, mark_send, mark_recv, full_send, full_recv, pack_send, pack_recv):
    heads, cubes, picks = idx_ref.shape
    rows = q_hbm.shape[0]
    depth = q_hbm.shape[1] // heads
    half = ring_size // 2
    whole = half - 3
    factor = math.log2(math.e) / math.sqrt(depth)
    me = lax.axis_index("seq")

    def away(distance):
        return lax.rem(me + distance + ring_size, ring_size)

    def source(way, distance):
        return away(-distance if way == RIGHT else distance)

    def target(way):
        return {"seq": away(1 if way == RIGHT else -1)}

    barrier = pltpu.get_barrier_semaphore()
    for distance in (1, -1, 2, -2):
        pl.semaphore_signal(barrier, inc=1, device_id={"seq": away(distance)},
                            device_id_type=pl.DeviceIdType.MESH)

    idx_load = pltpu.make_async_copy(idx_hbm, idx_ref, idx_sem)
    idx_load.start()
    loads = []
    for h in range(heads):
        columns = pl.ds(h * depth, depth)
        for part, ref in ((0, k_hbm), (1, v_hbm)):
            loads.append(pltpu.make_async_copy(
                ref.at[:, columns], ring.at[RIGHT, 0, h, part], kv_sem.at[h, part]))
            loads[-1].start()
    q_loads = []
    for h in range(heads):
        q_loads.append(pltpu.make_async_copy(
            q_hbm.at[:, pl.ds(h * depth, depth)], q_aug.at[h, :, pl.ds(0, depth)], q_sem.at[h]))
        q_loads[-1].start()

    def remote(src, dst, sends, recvs, device):
        return pltpu.make_async_remote_copy(
            src_ref=src, dst_ref=dst, send_sem=sends, recv_sem=recvs,
            device_id=device, device_id_type=pl.DeviceIdType.MESH)

    def hop(way, step, h):
        first = isinstance(step, int) and step == 0
        return remote(ring.at[RIGHT if first else way, step, h], ring.at[way, step + 1, h],
                      full_send.at[way, step, h], full_recv.at[way, step, h], target(way))

    def long_part(way):
        return 0 if way == RIGHT else 1

    def whole_long(way, h):
        part = long_part(way)
        return remote(ring.at[way, whole, h, part], ring.at[way, whole + 1, h, part],
                      full_send.at[way, whole, h], full_recv.at[way, whole, h], target(way))

    def pair_hop(way, kind, h):
        return remote(stage.at[way, kind, h], pairs.at[way, kind, h],
                      pack_send.at[way, kind, h, 0], pack_recv.at[way, kind, h, 0], target(way))

    def single_hop(way, kind, h):
        return remote(pairs.at[way, kind, h, 1], single.at[way, kind, h],
                      pack_send.at[way, kind, h, 1], pack_recv.at[way, kind, h, 1], target(way))

    def mark_hop(n):
        return remote(marks.at[0], marks.at[1 + (n ^ 1)], mark_send.at[n], mark_recv.at[n],
                      {"seq": away(NEAR[n])})

    pl.semaphore_wait(barrier, 4)
    for h in range(heads):
        loads[2 * h].wait()
        loads[2 * h + 1].wait()
        hop(RIGHT, 0, h).start()
        hop(LEFT, 0, h).start()

    lanes = lax.broadcasted_iota(jnp.int32, (cubes, LANES), 1)
    idx_load.wait()
    marks[0] = jnp.zeros(marks.shape[1:], jnp.float32)
    for h in range(heads):
        chosen = idx_ref[h]
        hit = jnp.zeros((cubes, LANES), jnp.float32)
        for j in range(picks):
            hit = jnp.where(chosen[:, j:j + 1] == lanes, 1.0, hit)
        marks[0, h:h + 1, :] = jnp.max(hit, axis=0, keepdims=True)
        bias = jnp.where(hit > 0.5, 0.0, MASKED)
        for c in range(cubes):
            q_aug[h, c * CUBE_TOK:(c + 1) * CUBE_TOK, depth:] = jnp.broadcast_to(
                bias[c:c + 1, :], (CUBE_TOK, LANES)).astype(q_aug.dtype)
    for n in range(len(NEAR)):
        mark_hop(n).start()
    top[...] = jnp.full(top.shape, MASKED, jnp.float32)
    tot[...] = jnp.zeros(tot.shape, jnp.float32)
    acc[...] = jnp.zeros(acc.shape, jnp.float32)

    shift = lax.shift_right_logical
    key_cube = shift(lax.broadcasted_iota(jnp.int32, (rows, LANES), 0), jnp.int32(6))
    key_lane = lax.broadcasted_iota(jnp.int32, (rows, LANES), 1)

    def one_hot(owner):
        return jnp.where(key_lane == key_cube + owner * cubes, 1.0, 0.0).astype(jnp.bfloat16)

    tile = min(rows, 256)

    def attend(h, blocks):
        for r in range(0, rows, tile):
            part = pl.ds(r, tile)
            scores = [
                lax.dot_general(q_aug[h, part, :], key, (((1,), (1,)), ((), ())),
                                preferred_element_type=jnp.float32)
                for key, _ in blocks
            ]
            peak = functools.reduce(
                jnp.maximum, [jnp.max(s, axis=1, keepdims=True) for s in scores])
            before = top[h, part, :]
            after = jnp.maximum(before, peak)
            scale = jnp.exp2((before - after) * factor)
            total = tot[h, part, :] * scale
            mixed = acc[h, part, :] * scale
            for s, (_, value) in zip(scores, blocks):
                pieces = []
                for c in range(0, s.shape[1], LANES):
                    w = jnp.exp2((s[:, c:c + LANES] - after) * factor)
                    total = total + w
                    pieces.append(w.astype(jnp.bfloat16))
                mixed = mixed + jnp.dot(jnp.concatenate(pieces, axis=1), value,
                                        preferred_element_type=jnp.float32)
            top[h, part, :] = after
            tot[h, part, :] = total
            acc[h, part, :] = mixed

    def whole_block(way, step, h, hot):
        return (jnp.concatenate([ring[way, step, h, 0], hot], axis=1), ring[way, step, h, 1])

    for h in range(heads):
        q_loads[h].wait()
    hot_own = one_hot(me)
    for h in range(heads):
        attend(h, [whole_block(RIGHT, 0, h, hot_own)])

    across = lax.broadcasted_iota(jnp.int32, (LANES, LANES), 1)
    down = lax.broadcasted_iota(jnp.int32, (LANES, LANES), 0)
    same = shift(across, jnp.int32(3)) == shift(down, jnp.int32(3))
    before_it = jnp.where(same & (down < across), 1.0, 0.0).astype(jnp.bfloat16)
    rank_row = jnp.dot(marks[0].astype(jnp.bfloat16), before_it, preferred_element_type=jnp.float32)
    mark_row = marks[0]
    weight = jnp.where(same & (across < down), 1.0, jnp.where(across == down, float(PICKED), 0.0))
    ones = jnp.ones((LANES, LANES), jnp.bfloat16)
    for n in range(len(NEAR)):
        mark_hop(n).wait_recv()
    for n in range(1 + len(NEAR)):
        for h in range(heads):
            tables[n, h] = jnp.dot((weight * marks[n, h:h + 1, :]).astype(jnp.bfloat16), ones,
                                   preferred_element_type=jnp.float32)

    def pick(n, h, owner, block):
        table = tables[n, h, pl.ds(pl.multiple_of(owner * cubes, cubes), cubes), :]
        out = [jnp.zeros((CUBE_TOK, depth), jnp.float32) for _ in range(KEEP)]
        for c in range(cubes):
            cube = block[c * CUBE_TOK:(c + 1) * CUBE_TOK, :].astype(jnp.float32)
            for r in range(KEEP):
                out[r] = jnp.where(table[c:c + 1, :] == float(PICKED + r), cube, out[r])
        return jnp.concatenate(out, axis=0).astype(jnp.bfloat16)

    lane = lax.broadcasted_iota(jnp.int32, (1, LANES), 1)

    def pack_hot(h, owner):
        inside = (shift(lane, jnp.int32(3)) == owner) & (mark_row[h:h + 1, :] > 0.5)
        out = []
        for r in range(KEEP):
            hot = jnp.where(inside & (rank_row[h:h + 1, :] == float(r)), 1.0, 0.0)
            found = jnp.max(hot, axis=1, keepdims=True)
            out.append(jnp.broadcast_to(jnp.where(found > 0.5, hot, 1.0), (CUBE_TOK, LANES)))
        return jnp.concatenate(out, axis=0).astype(jnp.bfloat16)

    def make_packs(way, kind, h, distance, part):
        owner = source(way, distance)
        block = ring[way, distance, h, part]
        first = 1 if way == RIGHT else 2
        stage[way, kind, h, 0] = pick(first, h, owner, block)
        stage[way, kind, h, 1] = pick(first + 2, h, owner, block)

    def body(step, carry):
        hots = [one_hot(source(way, step)) for way in (RIGHT, LEFT)]
        for h in range(heads):
            for way in (RIGHT, LEFT):
                hop(way, step - 1, h).wait_recv()
                hop(way, step, h).start()
            attend(h, [whole_block(way, step, h, hots[way]) for way in (RIGHT, LEFT)])
        return carry

    lax.fori_loop(1, whole, body, 0)

    hots = [one_hot(source(way, whole)) for way in (RIGHT, LEFT)]
    for h in range(heads):
        for way in (RIGHT, LEFT):
            hop(way, whole - 1, h).wait_recv()
            whole_long(way, h).start()
        for way in (RIGHT, LEFT):
            make_packs(way, SHORT, h, whole, 1 - long_part(way))
            pair_hop(way, SHORT, h).start()
        attend(h, [whole_block(way, whole, h, hots[way]) for way in (RIGHT, LEFT)])

    for h in range(heads):
        for way in (RIGHT, LEFT):
            whole_long(way, h).wait_recv()
            make_packs(way, LONG, h, whole + 1, long_part(way))
            pair_hop(way, LONG, h).start()
            pair_hop(way, SHORT, h).wait_recv()
            single_hop(way, SHORT, h).start()
        far_right, far_left = source(RIGHT, whole + 1), source(LEFT, whole + 1)
        keys = jnp.concatenate([pick(0, h, far_right, ring[RIGHT, whole + 1, h, 0]),
                                pairs[LEFT, SHORT, h, 0]], axis=0)
        hot = jnp.concatenate([pack_hot(h, far_right), pack_hot(h, far_left)], axis=0)
        values = jnp.concatenate([pairs[RIGHT, SHORT, h, 0],
                                  pick(0, h, far_left, ring[LEFT, whole + 1, h, 1])], axis=0)
        attend(h, [(jnp.concatenate([keys, hot], axis=1), values)])

    for h in range(heads):
        for way in (RIGHT, LEFT):
            pair_hop(way, LONG, h).wait_recv()
            single_hop(way, LONG, h).start()
            single_hop(way, SHORT, h).wait_recv()
        keys = jnp.concatenate([pairs[RIGHT, LONG, h, 0], single[LEFT, SHORT, h]], axis=0)
        hot = jnp.concatenate([pack_hot(h, source(RIGHT, whole + 2)),
                               pack_hot(h, source(LEFT, whole + 2))], axis=0)
        values = jnp.concatenate([single[RIGHT, SHORT, h], pairs[LEFT, LONG, h, 0]], axis=0)
        attend(h, [(jnp.concatenate([keys, hot], axis=1), values)])

    empty = jnp.zeros((CUBE_TOK, depth), jnp.bfloat16)
    for h in range(heads):
        hot = jnp.concatenate([pack_hot(h, away(half)), jnp.ones((CUBE_TOK, LANES), jnp.bfloat16)], axis=0)
        single_hop(RIGHT, LONG, h).wait_recv()
        single_hop(LEFT, LONG, h).wait_recv()
        keys = jnp.concatenate([single[RIGHT, LONG, h], empty], axis=0)
        values = jnp.concatenate([single[LEFT, LONG, h], empty], axis=0)
        attend(h, [(jnp.concatenate([keys, hot], axis=1), values)])
        total = jnp.sum(tot[h], axis=1, keepdims=True)
        out_ref[:, h * depth:(h + 1) * depth] = (acc[h] / total).astype(out_ref.dtype)

    for n in range(len(NEAR)):
        mark_hop(n).wait_send()
    for h in range(heads):
        for way in (RIGHT, LEFT):
            hop(way, 0, h).wait_send()
            whole_long(way, h).wait_send()
            for kind in (SHORT, LONG):
                pair_hop(way, kind, h).wait_send()
                single_hop(way, kind, h).wait_send()

    def drain(step, carry):
        for way in (RIGHT, LEFT):
            for h in range(heads):
                hop(way, step, h).wait_send()
        return carry

    lax.fori_loop(1, whole, drain, 0)


def body(ring_size, queries, keys, values, indices):
    heads, cubes, picks = indices.shape
    rows, width = queries.shape
    depth = width // heads
    half = ring_size // 2
    pack = KEEP * CUBE_TOK
    hbm = pl.BlockSpec(memory_space=pl.ANY)
    return pl.pallas_call(
        functools.partial(kernel, ring_size),
        out_shape=jax.ShapeDtypeStruct((rows, width), queries.dtype),
        in_specs=[hbm] * 4,
        out_specs=pl.BlockSpec(memory_space=pltpu.VMEM),
        scratch_shapes=[
            pltpu.VMEM((heads, rows, depth + LANES), jnp.bfloat16),
            pltpu.VMEM((2, half - 1, heads, 2, rows, depth), jnp.bfloat16),
            pltpu.VMEM((2, 2, heads, 2, pack, depth), jnp.bfloat16),
            pltpu.VMEM((2, 2, heads, 2, pack, depth), jnp.bfloat16),
            pltpu.VMEM((2, 2, heads, pack, depth), jnp.bfloat16),
            pltpu.VMEM((1 + len(NEAR), 8, LANES), jnp.float32),
            pltpu.VMEM((1 + len(NEAR), heads, LANES, LANES), jnp.float32),
            pltpu.VMEM((heads, cubes, picks), jnp.int32),
            pltpu.VMEM((heads, rows, depth), jnp.float32),
            pltpu.VMEM((heads, rows, LANES), jnp.float32),
            pltpu.VMEM((heads, rows, LANES), jnp.float32),
            pltpu.SemaphoreType.DMA((heads,)),
            pltpu.SemaphoreType.DMA((heads, 2)),
            pltpu.SemaphoreType.DMA,
            pltpu.SemaphoreType.DMA((len(NEAR),)),
            pltpu.SemaphoreType.DMA((len(NEAR),)),
            pltpu.SemaphoreType.DMA((2, half - 2, heads)),
            pltpu.SemaphoreType.DMA((2, half - 2, heads)),
            pltpu.SemaphoreType.DMA((2, 2, heads, 2)),
            pltpu.SemaphoreType.DMA((2, 2, heads, 2)),
        ],
        compiler_params=pltpu.CompilerParams(
            collective_id=0, has_side_effects=True, vmem_limit_bytes=63 * 2 ** 20),
        cost_estimate=pl.CostEstimate(
            flops=4 * rows * rows * ring_size * width,
            bytes_accessed=8 * rows * width,
            transcendentals=rows * rows * ring_size * heads),
        name="ring_attention",
    )(queries, keys, values, indices)


def solution(mesh):
    placed = (
        P(("dp", "seq"), "head"),
        P(("dp", "seq"), "head"),
        P(("dp", "seq"), "head"),
        P("head", ("dp", "seq"), None),
    )
    return jax.shard_map(
        functools.partial(body, mesh.shape["seq"]), mesh=mesh, in_specs=placed,
        out_specs=P(("dp", "seq"), "head"), check_vma=False,
    )
```

time: 145 us -> 132 us (0.910)
  the two profiles are of different devices: /device:TPU:30 before, /device:TPU:8 now
where the time goes in v2:
time: 132 us
  Pallas kernels  130 us (98%)
  local copies, waits for them, and re-layouts  1.78 us (1%)
    pallas_call x1, Pallas kernels, body(): pl.pallas_call(functools.partial(kernel, ring_size), out_shape=jax.ShapeD...  130 us

profile of v2, /device:TPU:8, one launch (start us, length us, event | category | flops | bytes accessed | tf_op | source)
XLA Modules:
  0.0 131.8 jit_solution(14545057868751368358)
XLA Ops:
  0.0 130.0 %ring_attention.1 = bf16[512,384]{1,0:T(8,128)(2,1)} custom-call(bf16[512,384]{1,0:T(8,128)(2,1)} %q_hbm.1, bf16[512,384]{1,0:T(8,128)(2,1)} %k_hbm.1, bf16[512,384]{1,0:T(8,128)(2,1)} %v_hbm.1, s32[3,8,32]{2,1,0:T(8,128)} %idx_hbm.1), custom_call_target="tpu_custom_call" | custom-call | flops 6442450944 | bytes 1572864 | tf_op jit(solution)/shard_map/ring_attention/pallas_call | solution.py:288
  130.0 1.8 %copy.6 = bf16[512,384]{1,0:T(8,128)(2,1)} copy(bf16[512,384]{1,0:T(8,128)(2,1)} %ring_attention.1) | data formatting | bytes 786432

commit v3 on v2

v3 whole, which is shorter than its diff:
```python
import functools
import math

import jax
import jax.numpy as jnp
from jax import lax
from jax.experimental import pallas as pl
from jax.experimental.pallas import tpu as pltpu
from jax.sharding import PartitionSpec as P

CUBE_TOK = 64
LIMIT = 53 * 2 ** 20 + 2 ** 19
LANES = 128
MASKED = -1e30
KEEP = 3
PICKED = 16
NEAR = (1, -1, 2, -2)
RIGHT, LEFT = 0, 1
K, V = 0, 1
SHORT, LONG = 0, 1
FAR_RIGHT = ((0xFDFF, 0xFDFF, 0xFDFF), (0x0080, 0x0080, 0x0080))


def kernel(ring_size, q_hbm, k_hbm, v_hbm, idx_hbm, out_ref,
           q_aug, ring, stage, pairs, single, mine, marks, tables, idx_ref, acc, top, tot,
           q_sem, kv_sem, idx_sem, mark_send, mark_recv, full_send, full_recv, pack_send, pack_recv):
    heads, cubes, picks = idx_ref.shape
    rows = q_hbm.shape[0]
    depth = q_hbm.shape[1] // heads
    half = ring_size // 2
    whole = half - 3
    factor = math.log2(math.e) / math.sqrt(depth)
    me = lax.axis_index("seq")

    def away(distance):
        return lax.rem(me + distance + ring_size, ring_size)

    def source(way, distance):
        return away(-distance if way == RIGHT else distance)

    def target(way):
        return {"seq": away(1 if way == RIGHT else -1)}

    barrier = pltpu.get_barrier_semaphore()
    for distance in (1, -1):
        pl.semaphore_signal(barrier, inc=1, device_id={"seq": away(distance)},
                            device_id_type=pl.DeviceIdType.MESH)

    idx_load = pltpu.make_async_copy(idx_hbm, idx_ref, idx_sem)
    idx_load.start()
    loads = []
    for h in range(heads):
        columns = pl.ds(h * depth, depth)
        for part, ref in ((0, k_hbm), (1, v_hbm)):
            loads.append(pltpu.make_async_copy(
                ref.at[:, columns], ring.at[RIGHT, 0, h, part], kv_sem.at[h, part]))
            loads[-1].start()
    q_loads = []
    for h in range(heads):
        q_loads.append(pltpu.make_async_copy(
            q_hbm.at[:, pl.ds(h * depth, depth)], q_aug.at[h, :, pl.ds(0, depth)], q_sem.at[h]))
        q_loads[-1].start()

    def remote(src, dst, sends, recvs, device):
        return pltpu.make_async_remote_copy(
            src_ref=src, dst_ref=dst, send_sem=sends, recv_sem=recvs,
            device_id=device, device_id_type=pl.DeviceIdType.MESH)

    def hop(way, step, h):
        first = isinstance(step, int) and step == 0
        return remote(ring.at[RIGHT if first else way, step, h], ring.at[way, step + 1, h],
                      full_send.at[way, step, h], full_recv.at[way, step, h], target(way))

    def goes_far(way, part, h, owner):
        bit = lax.rem(lax.shift_right_logical(jnp.int32(FAR_RIGHT[part][h]), owner), 2)
        return bit == (1 if way == RIGHT else 0)

    def whole_part(way, part, h):
        return remote(ring.at[way, whole, h, part], ring.at[way, whole + 1, h, part],
                      pack_send.at[way, part, h, 2], pack_recv.at[way, part, h, 2], target(way))

    def pair_hop(way, part, kind, h):
        return remote(stage.at[way, part, kind, h], pairs.at[way, part, kind, h],
                      pack_send.at[way, part, h, kind], pack_recv.at[way, part, h, kind], target(way))

    def single_hop(way, part, kind, h):
        return remote(pairs.at[way, part, kind, h, 1], single.at[way, part, kind, h],
                      pack_send.at[way, part, h, 3 + kind], pack_recv.at[way, part, h, 3 + kind], target(way))

    def mark_hop(n):
        return remote(marks.at[0 if n < 2 else 1 + ((n - 2) ^ 1)], marks.at[1 + (n ^ 1)],
                      mark_send.at[n], mark_recv.at[n], {"seq": away(NEAR[n % 2])})

    pl.semaphore_wait(barrier, 2)
    for h in range(heads):
        loads[2 * h].wait()
        loads[2 * h + 1].wait()
        hop(RIGHT, 0, h).start()
        hop(LEFT, 0, h).start()

    lanes = lax.broadcasted_iota(jnp.int32, (cubes, LANES), 1)
    idx_load.wait()
    marks[0] = jnp.zeros(marks.shape[1:], jnp.float32)
    for h in range(heads):
        chosen = idx_ref[h]
        hit = jnp.zeros((cubes, LANES), jnp.float32)
        for j in range(picks):
            hit = jnp.where(chosen[:, j:j + 1] == lanes, 1.0, hit)
        marks[0, h:h + 1, :] = jnp.max(hit, axis=0, keepdims=True)
        bias = jnp.where(hit > 0.5, 0.0, MASKED)
        for c in range(cubes):
            q_aug[h, c * CUBE_TOK:(c + 1) * CUBE_TOK, depth:] = jnp.broadcast_to(
                bias[c:c + 1, :], (CUBE_TOK, LANES)).astype(q_aug.dtype)
    for n in (0, 1):
        mark_hop(n).start()
    top[...] = jnp.full(top.shape, MASKED, jnp.float32)
    tot[...] = jnp.zeros(tot.shape, jnp.float32)
    acc[...] = jnp.zeros(acc.shape, jnp.float32)

    shift = lax.shift_right_logical
    key_cube = shift(lax.broadcasted_iota(jnp.int32, (rows, LANES), 0), jnp.int32(6))
    key_lane = lax.broadcasted_iota(jnp.int32, (rows, LANES), 1)

    def one_hot(owner):
        return jnp.where(key_lane == key_cube + owner * cubes, 1.0, 0.0).astype(jnp.bfloat16)

    tile = min(rows, 256)

    def attend(h, blocks):
        for r in range(0, rows, tile):
            part = pl.ds(r, tile)
            scores = [
                lax.dot_general(q_aug[h, part, :], key, (((1,), (1,)), ((), ())),
                                preferred_element_type=jnp.float32)
                for key, _ in blocks
            ]
            peak = functools.reduce(
                jnp.maximum, [jnp.max(s, axis=1, keepdims=True) for s in scores])
            before = top[h, part, :]
            after = jnp.maximum(before, peak)
            scale = jnp.exp2((before - after) * factor)
            total = tot[h, part, :] * scale
            mixed = acc[h, part, :] * scale
            for s, (_, value) in zip(scores, blocks):
                pieces = []
                for c in range(0, s.shape[1], LANES):
                    w = jnp.exp2((s[:, c:c + LANES] - after) * factor)
                    total = total + w
                    pieces.append(w.astype(jnp.bfloat16))
                mixed = mixed + jnp.dot(jnp.concatenate(pieces, axis=1), value,
                                        preferred_element_type=jnp.float32)
            top[h, part, :] = after
            tot[h, part, :] = total
            acc[h, part, :] = mixed

    def whole_block(way, step, h, hot):
        return (jnp.concatenate([ring[way, step, h, 0], hot], axis=1), ring[way, step, h, 1])

    for h in range(heads):
        q_loads[h].wait()
    hot_own = one_hot(me)
    for h in range(heads):
        attend(h, [whole_block(RIGHT, 0, h, hot_own)])

    def pick(n, h, owner, block):
        table = tables[n, h, pl.ds(pl.multiple_of(owner * cubes, cubes), cubes), :]
        out = [jnp.zeros((CUBE_TOK, depth), jnp.float32) for _ in range(KEEP)]
        for c in range(cubes):
            cube = block[c * CUBE_TOK:(c + 1) * CUBE_TOK, :].astype(jnp.float32)
            for r in range(KEEP):
                out[r] = jnp.where(table[c:c + 1, :] == float(PICKED + r), cube, out[r])
        return jnp.concatenate(out, axis=0).astype(jnp.bfloat16)

    lane = lax.broadcasted_iota(jnp.int32, (1, LANES), 1)

    def pack_hot(h, owner):
        inside = (shift(lane, jnp.int32(3)) == owner) & (mark_row[h:h + 1, :] > 0.5)
        out = []
        for r in range(KEEP):
            hot = jnp.where(inside & (rank_row[h:h + 1, :] == float(r)), 1.0, 0.0)
            found = jnp.max(hot, axis=1, keepdims=True)
            out.append(jnp.broadcast_to(jnp.where(found > 0.5, hot, 1.0), (CUBE_TOK, LANES)))
        return jnp.concatenate(out, axis=0).astype(jnp.bfloat16)

    def make_packs(way, part, kind, h, distance):
        owner = source(way, distance)
        block = ring[way, distance, h, part]
        first = 1 if way == RIGHT else 2
        stage[way, part, kind, h, 0] = pick(first, h, owner, block)
        stage[way, part, kind, h, 1] = pick(first + 2, h, owner, block)

    def either(condition, first, second):
        pl.when(condition)(first)
        pl.when(jnp.logical_not(condition))(second)

    def attend_packs(h, near, far):
        keys = jnp.concatenate([mine[RIGHT, K], mine[LEFT, K]], axis=0)
        values = jnp.concatenate([mine[RIGHT, V], mine[LEFT, V]], axis=0)
        hot = jnp.concatenate([pack_hot(h, near), pack_hot(h, far)], axis=0)
        attend(h, [(jnp.concatenate([keys, hot], axis=1), values)])

    def body(step, carry):
        @pl.when(step == 2)
        def _():
            for n in (0, 1):
                mark_hop(n).wait_recv()
            for n in (2, 3):
                mark_hop(n).start()

        hots = [one_hot(source(way, step)) for way in (RIGHT, LEFT)]
        for h in range(heads):
            for way in (RIGHT, LEFT):
                hop(way, step - 1, h).wait_recv()
                hop(way, step, h).start()
            attend(h, [whole_block(way, step, h, hots[way]) for way in (RIGHT, LEFT)])
        return carry

    lax.fori_loop(1, whole, body, 0)

    across = lax.broadcasted_iota(jnp.int32, (LANES, LANES), 1)
    down = lax.broadcasted_iota(jnp.int32, (LANES, LANES), 0)
    same = shift(across, jnp.int32(3)) == shift(down, jnp.int32(3))
    before_it = jnp.where(same & (down < across), 1.0, 0.0).astype(jnp.bfloat16)
    rank_row = jnp.dot(marks[0].astype(jnp.bfloat16), before_it, preferred_element_type=jnp.float32)
    mark_row = marks[0]
    weight = jnp.where(same & (across < down), 1.0, jnp.where(across == down, float(PICKED), 0.0))
    ones = jnp.ones((LANES, LANES), jnp.bfloat16)
    for n in (2, 3):
        mark_hop(n).wait_recv()
    for n in range(1 + len(NEAR)):
        for h in range(heads):
            tables[n, h] = jnp.dot((weight * marks[n, h:h + 1, :]).astype(jnp.bfloat16), ones,
                                   preferred_element_type=jnp.float32)

    hots = [one_hot(source(way, whole)) for way in (RIGHT, LEFT)]
    for h in range(heads):
        for way in (RIGHT, LEFT):
            hop(way, whole - 1, h).wait_recv()
            for part in (K, V):
                def on_whole(way=way, part=part, h=h):
                    whole_part(way, part, h).start()

                def as_packs(way=way, part=part, h=h):
                    make_packs(way, part, SHORT, h, whole)
                    pair_hop(way, part, SHORT, h).start()

                either(goes_far(way, part, h, source(way, whole)), on_whole, as_packs)
        attend(h, [whole_block(way, whole, h, hots[way]) for way in (RIGHT, LEFT)])

    for h in range(heads):
        for way in (RIGHT, LEFT):
            for part in (K, V):
                def from_whole(way=way, part=part, h=h):
                    whole_part(way, part, h).wait_recv()
                    make_packs(way, part, LONG, h, whole + 1)
                    pair_hop(way, part, LONG, h).start()
                    mine[way, part] = pick(0, h, source(way, whole + 1), ring[way, whole + 1, h, part])

                def from_pair(way=way, part=part, h=h):
                    pair_hop(way, part, SHORT, h).wait_recv()
                    single_hop(way, part, SHORT, h).start()
                    mine[way, part] = pairs[way, part, SHORT, h, 0]

                either(goes_far(way, part, h, source(way, whole + 1)), from_whole, from_pair)
        attend_packs(h, source(RIGHT, whole + 1), source(LEFT, whole + 1))

    for h in range(heads):
        for way in (RIGHT, LEFT):
            for part in (K, V):
                def from_pair(way=way, part=part, h=h):
                    pair_hop(way, part, LONG, h).wait_recv()
                    single_hop(way, part, LONG, h).start()
                    mine[way, part] = pairs[way, part, LONG, h, 0]

                def from_single(way=way, part=part, h=h):
                    single_hop(way, part, SHORT, h).wait_recv()
                    mine[way, part] = single[way, part, SHORT, h]

                either(goes_far(way, part, h, source(way, whole + 2)), from_pair, from_single)
        attend_packs(h, source(RIGHT, whole + 2), source(LEFT, whole + 2))

    for n in range(len(NEAR)):
        mark_hop(n).wait_send()
    for h in range(heads):
        for way in (RIGHT, LEFT):
            hop(way, 0, h).wait_send()
            for part in (K, V):
                either(goes_far(way, part, h, source(way, whole)),
                       whole_part(way, part, h).wait_send, pair_hop(way, part, SHORT, h).wait_send)
                either(goes_far(way, part, h, source(way, whole + 1)),
                       pair_hop(way, part, LONG, h).wait_send, single_hop(way, part, SHORT, h).wait_send)

    def drain(step, carry):
        for way in (RIGHT, LEFT):
            for h in range(heads):
                hop(way, step, h).wait_send()
        return carry

    lax.fori_loop(1, whole, drain, 0)

    empty = jnp.zeros((CUBE_TOK, depth), jnp.bfloat16)
    opposite = away(half)
    for h in range(heads):
        hot = jnp.concatenate([pack_hot(h, opposite), jnp.ones((CUBE_TOK, LANES), jnp.bfloat16)], axis=0)
        for part in (K, V):
            def from_left_side(part=part, h=h):
                single_hop(RIGHT, part, LONG, h).wait_recv()
                mine[RIGHT, part] = single[RIGHT, part, LONG, h]

            def from_right_side(part=part, h=h):
                single_hop(LEFT, part, LONG, h).wait_recv()
                mine[RIGHT, part] = single[LEFT, part, LONG, h]

            either(goes_far(RIGHT, part, h, opposite), from_left_side, from_right_side)
        keys = jnp.concatenate([mine[RIGHT, K], empty], axis=0)
        values = jnp.concatenate([mine[RIGHT, V], empty], axis=0)
        attend(h, [(jnp.concatenate([keys, hot], axis=1), values)])
        total = jnp.sum(tot[h], axis=1, keepdims=True)
        out_ref[:, h * depth:(h + 1) * depth] = (acc[h] / total).astype(out_ref.dtype)

    for h in range(heads):
        for way in (RIGHT, LEFT):
            for part in (K, V):
                pl.when(goes_far(way, part, h, source(way, whole + 2)))(single_hop(way, part, LONG, h).wait_send)


def body(ring_size, queries, keys, values, indices):
    heads, cubes, picks = indices.shape
    rows, width = queries.shape
    depth = width // heads
    half = ring_size // 2
    pack = KEEP * CUBE_TOK
    hbm = pl.BlockSpec(memory_space=pl.ANY)
    return pl.pallas_call(
        functools.partial(kernel, ring_size),
        out_shape=jax.ShapeDtypeStruct((rows, width), queries.dtype),
        in_specs=[hbm] * 4,
        out_specs=pl.BlockSpec(memory_space=pltpu.VMEM),
        scratch_shapes=[
            pltpu.VMEM((heads, rows, depth + LANES), jnp.bfloat16),
            pltpu.VMEM((2, half - 1, heads, 2, rows, depth), jnp.bfloat16),
            pltpu.VMEM((2, 2, 2, heads, 2, pack, depth), jnp.bfloat16),
            pltpu.VMEM((2, 2, 2, heads, 2, pack, depth), jnp.bfloat16),
            pltpu.VMEM((2, 2, 2, heads, pack, depth), jnp.bfloat16),
            pltpu.VMEM((2, 2, pack, depth), jnp.bfloat16),
            pltpu.VMEM((1 + len(NEAR), 8, LANES), jnp.float32),
            pltpu.VMEM((1 + len(NEAR), heads, LANES, LANES), jnp.float32),
            pltpu.VMEM((heads, cubes, picks), jnp.int32),
            pltpu.VMEM((heads, rows, depth), jnp.float32),
            pltpu.VMEM((heads, rows, LANES), jnp.float32),
            pltpu.VMEM((heads, rows, LANES), jnp.float32),
            pltpu.SemaphoreType.DMA((heads,)),
            pltpu.SemaphoreType.DMA((heads, 2)),
            pltpu.SemaphoreType.DMA,
            pltpu.SemaphoreType.DMA((len(NEAR),)),
            pltpu.SemaphoreType.DMA((len(NEAR),)),
            pltpu.SemaphoreType.DMA((2, half - 3, heads)),
            pltpu.SemaphoreType.DMA((2, half - 3, heads)),
            pltpu.SemaphoreType.DMA((2, 2, heads, 5)),
            pltpu.SemaphoreType.DMA((2, 2, heads, 5)),
        ],
        compiler_params=pltpu.CompilerParams(
            collective_id=0, has_side_effects=True, vmem_limit_bytes=LIMIT),
        cost_estimate=pl.CostEstimate(
            flops=4 * rows * rows * ring_size * width,
            bytes_accessed=8 * rows * width,
            transcendentals=rows * rows * ring_size * heads),
        name="ring_attention",
    )(queries, keys, values, indices)


def solution(mesh):
    placed = (
        P(("dp", "seq"), "head"),
        P(("dp", "seq"), "head"),
        P(("dp", "seq"), "head"),
        P("head", ("dp", "seq"), None),
    )
    return jax.shard_map(
        functools.partial(body, mesh.shape["seq"]), mesh=mesh, in_specs=placed,
        out_specs=P(("dp", "seq"), "head"), check_vma=False,
    )
```

time: 132 us -> 127 us (0.962)
  the two profiles are of different devices: /device:TPU:8 before, /device:TPU:26 now
where the time goes in v3:
time: 127 us
  Pallas kernels  126 us (99%)
  local copies, waits for them, and re-layouts  1.45 us (1%)
    pallas_call x1, Pallas kernels, body(): pl.pallas_call(functools.partial(kernel, ring_size), out_shape=jax.ShapeD...  126 us

profile of v3, /device:TPU:26, one launch (start us, length us, event | category | flops | bytes accessed | tf_op | source)
XLA Modules:
  0.0 127.2 jit_solution(18415722723996157705)
XLA Ops:
  0.0 0.0 copy-start
  0.0 0.7 copy-done
  0.7 125.7 %ring_attention.1 = bf16[512,384]{1,0:T(8,128)(2,1)S(1)} custom-call(bf16[512,384]{1,0:T(8,128)(2,1)} %q_hbm.1, bf16[512,384]{1,0:T(8,128)(2,1)} %k_hbm.1, bf16[512,384]{1,0:T(8,128)(2,1)} %v_hbm.1, s32[3,8,32]{2,1,0:T(8,128)S(1)} %copy-done), custom_call_target="tpu_custom_call" | custom-call | flops 6442450944 | bytes 1572864 | tf_op jit(solution)/shard_map/ring_attention/pallas_call | solution.py:334
  126.5 0.7 copy.6
Async XLA Ops:
  0.0 0.7 copy-start

commit v4 on v3

--- a/solution.py
+++ b/solution.py
@@ -9,7 +9,7 @@
 from jax.sharding import PartitionSpec as P
 
 CUBE_TOK = 64
-LIMIT = 53 * 2 ** 20 + 2 ** 19
+LIMIT = 56 * 2 ** 20
 LANES = 128
 MASKED = -1e30
 KEEP = 3
@@ -18,7 +18,8 @@
 RIGHT, LEFT = 0, 1
 K, V = 0, 1
 SHORT, LONG = 0, 1
-FAR_RIGHT = ((0xFDFF, 0xFDFF, 0xFDFF), (0x0080, 0x0080, 0x0080))
+LEFT_FIRST = 5
+FAR_RIGHT = ((0x1856, 0xDFFC, 0xD95C), (0xE062, 0x8463, 0x9222))
 
 
 def kernel(ring_size, q_hbm, k_hbm, v_hbm, idx_hbm, out_ref,
@@ -31,15 +32,17 @@
     whole = half - 3
     factor = math.log2(math.e) / math.sqrt(depth)
     me = lax.axis_index("seq")
+    early = jnp.where(me < LEFT_FIRST, LEFT, RIGHT)
+    ways = (early, 1 - early)
 
     def away(distance):
         return lax.rem(me + distance + ring_size, ring_size)
 
     def source(way, distance):
-        return away(-distance if way == RIGHT else distance)
+        return away(distance * (2 * way - 1))
 
     def target(way):
-        return {"seq": away(1 if way == RIGHT else -1)}
+        return {"seq": away(1 - 2 * way)}
 
     barrier = pltpu.get_barrier_semaphore()
     for distance in (1, -1):
@@ -73,7 +76,7 @@
 
     def goes_far(way, part, h, owner):
         bit = lax.rem(lax.shift_right_logical(jnp.int32(FAR_RIGHT[part][h]), owner), 2)
-        return bit == (1 if way == RIGHT else 0)
+        return bit == 1 - way
 
     def whole_part(way, part, h):
         return remote(ring.at[way, whole, h, part], ring.at[way, whole + 1, h, part],
@@ -185,7 +188,7 @@
     def make_packs(way, part, kind, h, distance):
         owner = source(way, distance)
         block = ring[way, distance, h, part]
-        first = 1 if way == RIGHT else 2
+        first = 1 + way
         stage[way, part, kind, h, 0] = pick(first, h, owner, block)
         stage[way, part, kind, h, 1] = pick(first + 2, h, owner, block)
 
@@ -209,7 +212,7 @@
 
         hots = [one_hot(source(way, step)) for way in (RIGHT, LEFT)]
         for h in range(heads):
-            for way in (RIGHT, LEFT):
+            for way in ways:
                 hop(way, step - 1, h).wait_recv()
                 hop(way, step, h).start()
             attend(h, [whole_block(way, step, h, hots[way]) for way in (RIGHT, LEFT)])
@@ -234,7 +237,7 @@
 
     hots = [one_hot(source(way, whole)) for way in (RIGHT, LEFT)]
     for h in range(heads):
-        for way in (RIGHT, LEFT):
+        for way in ways:
             hop(way, whole - 1, h).wait_recv()
             for part in (K, V):
                 def on_whole(way=way, part=part, h=h):
@@ -248,7 +251,7 @@
         attend(h, [whole_block(way, whole, h, hots[way]) for way in (RIGHT, LEFT)])
 
     for h in range(heads):
-        for way in (RIGHT, LEFT):
+        for way in ways:
             for part in (K, V):
                 def from_whole(way=way, part=part, h=h):
                     whole_part(way, part, h).wait_recv()
@@ -265,7 +268,7 @@
         attend_packs(h, source(RIGHT, whole + 1), source(LEFT, whole + 1))
 
     for h in range(heads):
-        for way in (RIGHT, LEFT):
+        for way in ways:
             for part in (K, V):
                 def from_pair(way=way, part=part, h=h):
                     pair_hop(way, part, LONG, h).wait_recv()
@@ -333,7 +336,7 @@
     hbm = pl.BlockSpec(memory_space=pl.ANY)
     return pl.pallas_call(
         functools.partial(kernel, ring_size),
-        out_shape=jax.ShapeDtypeStruct((rows, width), queries.dtype),
+        out_shape=pltpu.VMEM((rows, width), queries.dtype),
         in_specs=[hbm] * 4,
         out_specs=pl.BlockSpec(memory_space=pltpu.VMEM),
         scratch_shapes=[

time: 127 us -> 125 us (0.984)
  the two profiles are of different devices: /device:TPU:26 before, /device:TPU:30 now
where the time goes in v4:
time: 125 us
  Pallas kernels  125 us (100%)
    pallas_call x1, Pallas kernels, body(): pl.pallas_call(functools.partial(kernel, ring_size), out_shape=pltpu.VMEM...  125 us

profile of v4, /device:TPU:30, one launch (start us, length us, event | category | flops | bytes accessed | tf_op | source)
XLA Modules:
  0.0 125.3 jit_solution(12420339825442424128)
XLA Ops:
  0.0 124.6 %ring_attention.1 = bf16[512,384]{1,0:T(8,128)(2,1)S(1)} custom-call(bf16[512,384]{1,0:T(8,128)(2,1)} %q_hbm.1, bf16[512,384]{1,0:T(8,128)(2,1)} %k_hbm.1, bf16[512,384]{1,0:T(8,128)(2,1)} %v_hbm.1, s32[3,8,32]{2,1,0:T(8,128)} %idx_hbm.1), custom_call_target="tpu_custom_call" | custom-call | flops 6442450944 | bytes 1572864 | tf_op jit(solution)/shard_map/ring_attention/pallas_call | solution.py:337
  124.6 0.7 copy.6

commit v5 on v4

--- a/solution.py
+++ b/solution.py
@@ -19,12 +19,13 @@
 K, V = 0, 1
 SHORT, LONG = 0, 1
 LEFT_FIRST = 5
-FAR_RIGHT = ((0x1856, 0xDFFC, 0xD95C), (0xE062, 0x8463, 0x9222))
+FAR_RIGHT = ((0x6073, 0xE973, 0x4123), (0x5CCC, 0x9CCC, 0xBC88))
 
 
 def kernel(ring_size, q_hbm, k_hbm, v_hbm, idx_hbm, out_ref,
            q_aug, ring, stage, pairs, single, mine, marks, tables, idx_ref, acc, top, tot,
-           q_sem, kv_sem, idx_sem, mark_send, mark_recv, full_send, full_recv, pack_send, pack_recv):
+           q_sem, kv_sem, idx_sem, mark_send, mark_recv, full_send, full_recv, pack_send, pack_recv,
+           answer_right, answer_left):
     heads, cubes, picks = idx_ref.shape
     rows = q_hbm.shape[0]
     depth = q_hbm.shape[1] // heads
@@ -44,10 +45,21 @@
     def target(way):
         return {"seq": away(1 - 2 * way)}
 
+    first_one, last_one, late = me == 0, me == ring_size - 1, me >= half
+
+    def tell(semaphore, distance):
+        pl.semaphore_signal(semaphore, inc=1, device_id={"seq": away(distance)},
+                            device_id_type=pl.DeviceIdType.MESH)
+
     barrier = pltpu.get_barrier_semaphore()
-    for distance in (1, -1):
-        pl.semaphore_signal(barrier, inc=1, device_id={"seq": away(distance)},
-                            device_id_type=pl.DeviceIdType.MESH)
+
+    @pl.when(jnp.logical_not(last_one))
+    def _():
+        tell(barrier, 1)
+
+    @pl.when(first_one | (me > half))
+    def _():
+        tell(barrier, -1)
 
     idx_load = pltpu.make_async_copy(idx_hbm, idx_ref, idx_sem)
     idx_load.start()
@@ -94,12 +106,37 @@
         return remote(marks.at[0 if n < 2 else 1 + ((n - 2) ^ 1)], marks.at[1 + (n ^ 1)],
                       mark_send.at[n], mark_recv.at[n], {"seq": away(NEAR[n % 2])})
 
-    pl.semaphore_wait(barrier, 2)
-    for h in range(heads):
-        loads[2 * h].wait()
-        loads[2 * h + 1].wait()
-        hop(RIGHT, 0, h).start()
-        hop(LEFT, 0, h).start()
+    @pl.when(jnp.logical_not(first_one))
+    def _():
+        pl.semaphore_wait(barrier, jnp.where(late, 2, 1))
+
+    @pl.when(jnp.logical_not(first_one) & (me <= half))
+    def _():
+        tell(answer_right, -1)
+
+    @pl.when(last_one)
+    def _():
+        tell(answer_left, 1)
+
+    for load in loads:
+        load.wait()
+
+    @pl.when(late)
+    def _():
+        for h in range(heads):
+            hop(RIGHT, 0, h).start()
+            hop(LEFT, 0, h).start()
+
+    @pl.when(jnp.logical_not(late))
+    def _():
+        @pl.when(jnp.logical_not(first_one))
+        def _():
+            for h in range(heads):
+                hop(LEFT, 0, h).start()
+
+        pl.semaphore_wait(answer_right, 1)
+        for h in range(heads):
+            hop(RIGHT, 0, h).start()
 
     lanes = lax.broadcasted_iota(jnp.int32, (cubes, LANES), 1)
     idx_load.wait()
@@ -114,8 +151,6 @@
         for c in range(cubes):
             q_aug[h, c * CUBE_TOK:(c + 1) * CUBE_TOK, depth:] = jnp.broadcast_to(
                 bias[c:c + 1, :], (CUBE_TOK, LANES)).astype(q_aug.dtype)
-    for n in (0, 1):
-        mark_hop(n).start()
     top[...] = jnp.full(top.shape, MASKED, jnp.float32)
     tot[...] = jnp.zeros(tot.shape, jnp.float32)
     acc[...] = jnp.zeros(acc.shape, jnp.float32)
@@ -201,6 +236,15 @@
         values = jnp.concatenate([mine[RIGHT, V], mine[LEFT, V]], axis=0)
         hot = jnp.concatenate([pack_hot(h, near), pack_hot(h, far)], axis=0)
         attend(h, [(jnp.concatenate([keys, hot], axis=1), values)])
+
+    @pl.when(first_one)
+    def _():
+        pl.semaphore_wait(answer_left, 1)
+        for h in range(heads):
+            hop(LEFT, 0, h).start()
+
+    for n in (0, 1):
+        mark_hop(n).start()
 
     def body(step, carry):
         @pl.when(step == 2)
@@ -361,6 +405,8 @@
             pltpu.SemaphoreType.DMA((2, half - 3, heads)),
             pltpu.SemaphoreType.DMA((2, 2, heads, 5)),
             pltpu.SemaphoreType.DMA((2, 2, heads, 5)),
+            pltpu.SemaphoreType.REGULAR,
+            pltpu.SemaphoreType.REGULAR,
         ],
         compiler_params=pltpu.CompilerParams(
             collective_id=0, has_side_effects=True, vmem_limit_bytes=LIMIT),

time: 125 us -> 126 us (level)
  no operation moved by 1% of the time
where the time goes in v5:
time: 126 us; the launch traced here: 125 us
  Pallas kernels  125 us (99%)
    pallas_call x1, Pallas kernels, body(): pl.pallas_call(functools.partial(kernel, ring_size), out_shape=pltpu.VMEM...  125 us

profile of v5, /device:TPU:30, one launch (start us, length us, event | category | flops | bytes accessed | tf_op | source)
XLA Modules:
  0.0 125.5 jit_solution(3346944427007714319)
XLA Ops:
  0.0 124.7 %ring_attention.1 = bf16[512,384]{1,0:T(8,128)(2,1)S(1)} custom-call(bf16[512,384]{1,0:T(8,128)(2,1)} %q_hbm.1, bf16[512,384]{1,0:T(8,128)(2,1)} %k_hbm.1, bf16[512,384]{1,0:T(8,128)(2,1)} %v_hbm.1, s32[3,8,32]{2,1,0:T(8,128)} %idx_hbm.1), custom_call_target="tpu_custom_call" | custom-call | flops 6442450944 | bytes 1572864 | tf_op jit(solution)/shard_map/ring_attention/pallas_call | solution.py:381
  124.7 0.7 copy.6

commit v6 on v4

--- a/solution.py
+++ b/solution.py
@@ -327,6 +327,12 @@
                 pl.when(goes_far(way, part, h, source(way, whole + 2)))(single_hop(way, part, LONG, h).wait_send)
 
 
+def hand_out(result, out, sem):
+    copy = pltpu.make_async_copy(result, out, sem)
+    copy.start()
+    copy.wait()
+
+
 def body(ring_size, queries, keys, values, indices):
     heads, cubes, picks = indices.shape
     rows, width = queries.shape
@@ -334,7 +340,7 @@
     half = ring_size // 2
     pack = KEEP * CUBE_TOK
     hbm = pl.BlockSpec(memory_space=pl.ANY)
-    return pl.pallas_call(
+    attended = pl.pallas_call(
         functools.partial(kernel, ring_size),
         out_shape=pltpu.VMEM((rows, width), queries.dtype),
         in_specs=[hbm] * 4,
@@ -370,6 +376,15 @@
             transcendentals=rows * rows * ring_size * heads),
         name="ring_attention",
     )(queries, keys, values, indices)
+    return pl.pallas_call(
+        hand_out,
+        out_shape=jax.ShapeDtypeStruct((rows, width), queries.dtype),
+        in_specs=[pl.BlockSpec(memory_space=pltpu.VMEM)],
+        out_specs=hbm,
+        scratch_shapes=[pltpu.SemaphoreType.DMA],
+        cost_estimate=pl.CostEstimate(flops=0, bytes_accessed=2 * rows * width, transcendentals=0),
+        name="hand_out",
+    )(attended)
 
 
 def solution(mesh):

time: 125 us -> 127 us (1.016)
    pallas_call x0 -> x1, Pallas kernels: none -> 1.75 us  [body(): pl.pallas_call(hand_out, out_shape=jax.ShapeDtypeStruct((rows, width), qu...]
where the time goes in v6:
time: 127 us
  Pallas kernels  126 us (99%)
    pallas_call x1, Pallas kernels, body(): pl.pallas_call(functools.partial(kernel, ring_size), out_shape=pltpu.VMEM...  125 us

profile of v6, /device:TPU:30, one launch (start us, length us, event | category | flops | bytes accessed | tf_op | source)
XLA Modules:
  0.0 127.2 jit_solution(12518441127971571045)
XLA Ops:
  0.0 124.6 %ring_attention.1.result = bf16[512,384]{1,0:T(8,128)(2,1)S(1)} custom-call(bf16[512,384]{1,0:T(8,128)(2,1)} %q_hbm.1, bf16[512,384]{1,0:T(8,128)(2,1)} %k_hbm.1, bf16[512,384]{1,0:T(8,128)(2,1)} %v_hbm.1, s32[3,8,32]{2,1,0:T(8,128)} %idx_hbm.1), custom_call_target="tpu_custom_call" | custom-call | flops 6442450944 | bytes 1572864 | tf_op jit(solution)/shard_map/ring_attention/pallas_call | solution.py:343
  124.6 0.0 copy-start
  124.6 0.7 copy-done
  125.3 1.7 %hand_out.1 = bf16[512,384]{1,0:T(8,128)(2,1)} custom-call(bf16[512,384]{1,0:T(8,128)(2,1)} %copy-done), custom_call_target="tpu_custom_call" | custom-call | bytes 393216 | tf_op jit(solution)/shard_map/hand_out/pallas_call | solution.py:379
Async XLA Ops:
  124.6 0.7 copy-start
